TPU v7x, 32 devices: a whole 2x2x4 slice. The times are simulated.
32 devices in a mesh: dp: 2 (over x), seq: 4 (over y, core), head: 4 (over z).
Axes of the slice: x: 2, y: 2, z: 4, core: 2. Of those that a mesh axis runs over, the one named last changes fastest.
Arguments:
- x_in: bfloat16 [2, 3072, 4096], P('dp', 'seq', 'head'), may hold values from -6 to 6
- b_in: bfloat16 [2, 3072, 1024], P('dp', 'seq', 'head'), may hold values from -6 to 6
- c_in: bfloat16 [2, 3072, 1024], P('dp', 'seq', 'head'), may hold values from -6 to 6
- z_in: bfloat16 [2, 3072, 4096], P('dp', 'seq', 'head'), may hold values from -24 to 24
- dt_in: float32 [2, 64, 3072], P('dp', 'head', 'seq'), may hold values from -10 to 4.5
- a_log: float32 [64], P('head'), may hold values from -2.3 to 0.58
- skip_gain: float32 [64], P('head'), may hold values from 0.5 to 1.5
- norm_gain: float32 [4096], P('head'), may hold values from 0.5 to 1.5
- conv_x: float32 [4, 4096], P(None, 'head'), may hold values from -3 to 3
- conv_b: float32 [4, 1024], P(None, 'head'), may hold values from -3 to 3
- conv_c: float32 [4, 1024], P(None, 'head'), may hold values from -3 to 3
- init_state: float32 [2, 64, 64, 128], P('dp', 'head'), may hold values from -0.5 to 0.5
- out_weight: bfloat16 [4096, 8192], P(('dp', 'seq'), 'head'), may hold values from -0.09375 to 0.09375
Outputs:
- mixed: bfloat16 [2, 3072, 8192], P('dp', 'seq', 'head')
All inputs are finite; a program needn't handle non-finite values.
Results may differ from a plain program's by a relative error of at most 0.0058.
Values may be sent and summed in bfloat16 or wider, within the bound.
A program may use at most 128 MiB of HBM per device.

v0:
```python
import jax
import jax.numpy as jnp
from jax import lax
from jax.sharding import PartitionSpec as P

HEAD_SIZE = 64
STATE = 128
BLOCK_LEN = 256
TAPS = 4


EPSILON = 1e-05


def from_behind(block, axis, distance):
    devices = range(lax.axis_size(axis))
    route = [(i - distance, i) for i in devices if i - distance in devices]
    return lax.ppermute(block, axis, route)


def entering(value, axis, join, neutral):
    count, mine = (lax.axis_size(axis), lax.axis_index(axis))
    pieces = jax.tree.map(lambda part: lax.all_gather(part, axis), value)
    subtotal = jax.tree.map(
        lambda part, zero: jnp.full_like(part, 0) + jnp.asarray(zero, part.dtype), value, neutral
    )

    def step(position, subtotal):
        longer = join(subtotal, jax.tree.map(lambda part: part[position], pieces))
        return jax.tree.map(lambda new, old: jnp.where(position < mine, new, old), longer, subtotal)

    return lax.fori_loop(0, count - 1, step, subtotal)


def causal_conv(signal, before, weight):
    joined = jnp.concatenate([before, signal], axis=1).astype(jnp.float32)
    length = signal.shape[1]
    tap_count = weight.shape[0]
    accum_total = weight[0] * joined[:, 0:length]
    for offset in range(1, tap_count):
        accum_total = accum_total + weight[offset] * joined[:, offset : offset + length]
    return jax.nn.silu(accum_total).astype(jnp.bfloat16)


def combine_states(first_pair, second_pair):
    return (
        first_pair[0] * second_pair[0],
        second_pair[0][..., None, None] * first_pair[1] + second_pair[1],
    )


def local(
    x_in,
    b_in,
    c_in,
    z_in,
    dt_in,
    a_log,
    skip_gain,
    norm_gain,
    conv_x,
    conv_b,
    conv_c,
    init_state,
    out_weight,
):
    highest = lax.Precision.HIGHEST
    roll_count, tok_count, wide_x = x_in.shape
    wide_b = b_in.shape[2]
    head_count = dt_in.shape[1]
    group_count = wide_b // STATE
    per_group = head_count // group_count
    block_count = tok_count // BLOCK_LEN
    rim_width = TAPS - 1
    edge_rows = jnp.concatenate(
        [
            x_in[:, tok_count - rim_width :],
            b_in[:, tok_count - rim_width :],
            c_in[:, tok_count - rim_width :],
        ],
        axis=2,
    )
    before = from_behind(edge_rows, "seq", 1)
    x_conv = causal_conv(x_in, before[:, :, :wide_x], conv_x)
    b_conv = causal_conv(b_in, before[:, :, wide_x : wide_x + wide_b], conv_b)
    c_conv = causal_conv(c_in, before[:, :, wide_x + wide_b :], conv_c)
    grouped = (roll_count, group_count, per_group, block_count, BLOCK_LEN)
    step_flat = jax.nn.softplus(dt_in)
    decay_rate = -jnp.exp(a_log)
    cum_decay = jnp.cumsum((step_flat * decay_rate[None, :, None]).reshape(grouped), axis=-1)
    step_size = step_flat.reshape(grouped)
    x_shaped = x_conv.reshape(roll_count, block_count, BLOCK_LEN, group_count, per_group, HEAD_SIZE)
    b_shaped = b_conv.reshape(roll_count, block_count, BLOCK_LEN, group_count, STATE)
    c_shaped = c_conv.reshape(roll_count, block_count, BLOCK_LEN, group_count, STATE)
    scores = jnp.einsum(
        "rcqgn,rcsgn->rgcqs", c_shaped, b_shaped, preferred_element_type=jnp.float32
    )
    query_pos = lax.broadcasted_iota(jnp.int32, (BLOCK_LEN, BLOCK_LEN), 0)
    key_pos = lax.broadcasted_iota(jnp.int32, (BLOCK_LEN, BLOCK_LEN), 1)
    causal = query_pos >= key_pos
    spread = cum_decay[..., :, None] - cum_decay[..., None, :]
    decay_mat = jnp.where(causal, jnp.exp(jnp.minimum(spread, 0.0)), jnp.float32(0.0))
    mixing = (scores[:, :, None] * decay_mat * step_size[..., None, :]).astype(jnp.bfloat16)
    intra_out = jnp.einsum(
        "rgkcqs,rcsgkp->rcqgkp", mixing, x_shaped, preferred_element_type=jnp.float32
    )
    last_decay = cum_decay[..., -1:]
    weights_in = jnp.exp(last_decay - cum_decay) * step_size
    weighted = (
        jnp.transpose(weights_in, (0, 3, 4, 1, 2))[..., None] * x_shaped.astype(jnp.float32)
    ).astype(jnp.bfloat16)
    block_states = jnp.einsum(
        "rcsgkp,rcsgn->rgkcpn", weighted, b_shaped, preferred_element_type=jnp.float32
    )
    block_decay = jnp.exp(last_decay[..., 0])
    running = jnp.zeros((roll_count, group_count, per_group, HEAD_SIZE, STATE), jnp.float32)
    carried = jnp.ones((roll_count, group_count, per_group), jnp.float32)
    starts = []
    factors = []
    for block_index in range(block_count):
        starts.append(running)
        factors.append(carried)
        running = (
            block_decay[..., block_index, None, None] * running + block_states[:, :, :, block_index]
        )
        carried = carried * block_decay[..., block_index]
    prefix_decay, prefix_state = entering(
        (carried, running), "seq", combine_states, (jnp.ones_like(carried), jnp.zeros_like(running))
    )
    incoming = prefix_state + prefix_decay[..., None, None] * init_state.reshape(
        roll_count, group_count, per_group, HEAD_SIZE, STATE
    )
    start_states = jnp.stack(
        [
            factors[block_index][..., None, None] * incoming + starts[block_index]
            for block_index in range(block_count)
        ],
        axis=3,
    )
    c_float = c_shaped.astype(jnp.float32)
    inter_out = jnp.einsum("rcqgn,rgkcpn->rcqgkp", c_float, start_states, precision=highest)
    inter_out = inter_out * jnp.transpose(jnp.exp(cum_decay), (0, 3, 4, 1, 2))[..., None]
    skip_shaped = skip_gain.reshape(group_count, per_group)[:, :, None]
    ssm_out = (intra_out + inter_out + skip_shaped * x_shaped.astype(jnp.float32)).reshape(
        roll_count, tok_count, group_count, per_group * HEAD_SIZE
    )
    gate_act = jax.nn.silu(z_in.astype(jnp.float32)).reshape(
        roll_count, tok_count, group_count, per_group * HEAD_SIZE
    )
    gated_out = ssm_out * gate_act
    mean_sq = jnp.mean(gated_out * gated_out, axis=-1, keepdims=True)
    normed = (
        gated_out
        * lax.rsqrt(mean_sq + EPSILON)
        * norm_gain.reshape(group_count, per_group * HEAD_SIZE)
    )
    normed = normed.astype(jnp.bfloat16).reshape(roll_count * tok_count, wide_x)
    wide_all = lax.all_gather(normed, "head", axis=1, tiled=True)
    full_weight = lax.all_gather(out_weight, ("dp", "seq"), axis=0, tiled=True)
    mixed_terms = jnp.dot(wide_all, full_weight, preferred_element_type=jnp.float32)
    return mixed_terms.astype(jnp.bfloat16).reshape(roll_count, tok_count, -1)


def solution(mesh):
    in_specs = (
        P("dp", "seq", "head"),
        P("dp", "seq", "head"),
        P("dp", "seq", "head"),
        P("dp", "seq", "head"),
        P("dp", "head", "seq"),
        P("head"),
        P("head"),
        P("head"),
        P(None, "head"),
        P(None, "head"),
        P(None, "head"),
        P("dp", "head", None, None),
        P(("dp", "seq"), "head"),
    )
    out_specs = P("dp", "seq", "head")
    return jax.shard_map(local, mesh=mesh, in_specs=in_specs, out_specs=out_specs, check_vma=False)
```

profile of v0, /device:TPU:5, one launch (start us, length us, event | category | flops | bytes accessed | tf_op | source)
XLA Modules:
  0.0 322.1 jit_solution(8432786643580266315)
XLA Ops:
  6.5 0.7 slice.121
  7.3 0.7 slice.122
  8.0 0.7 slice.123
  8.7 1.0 copy.153
  9.6 1.3 collective-permute-start
  10.9 0.7 exponential_negate_fusion
  11.6 0.9 broadcast_multiply_fusion
  12.5 3.4 %reduce-window.6 = f32[1,2,8,3,2,128]{5,2,3,4,1,0:T(8,128)S(1)} reduce-window(f32[1,2,8,3,2,128]{5,2,3,4,1,0:T(8,128)S(1)} %copy.159, f32[]{:T(128)} %constant.45.clone.1), window={size=1x1x1x1x1x128 pad=0_0x0_0x0_0x0_0x0_0x127_0}, to_apply=%region_0.1 | reduce-window | flops 1560576 | bytes 98308 | tf_op jit(solution)/shard_map/reduce-window
  15.9 0.1 slice.174
  16.0 0.1 copy.161
  16.2 0.5 copy.169
  16.7 0.2 broadcast.179
  16.9 0.7 exponential_bitcast_fusion
  17.6 0.4 copy.170
  18.1 0.6 slice_bitcast_fusion.3
  18.8 0.6 multiply_bitcast_fusion
  19.3 0.6 fusion.49
  19.9 1.7 copy.154
  21.6 0.4 copy.172
  22.0 1.0 slice.159
  23.0 0.8 maximum_convert_fusion
  23.8 3.5 %multiply_convert_fusion.3 = bf16[1,768,1024]{1,2,0:T(8,128)(2,1)S(1)} fusion(f32[1,771,1024]{1,2,0:T(8,128)S(1)} %maximum_convert_fusion, f32[1024]{0:T(1024)S(1)} %bitcast.170, f32[1024]{0:T(1024)S(1)} %bitcast.171, f32[1024]{0:T(1024)S(1)} %bitcast.169, f32[1024]{0:T(1024)S(1)} %bitcast.168), kind=kLoop, calls=%fused_computation.37 | loop fusion | flops 9437184 | bytes 14172160 | tf_op jit(solution)/shard_map/convert_element_type | solution.py:42
  27.3 2.2 reshape.545
  29.5 0.9 fusion.50
  30.4 0.1 copy.156
  30.5 0.1 maximum_convert_fusion.2
  30.6 0.5 multiply_convert_fusion.4
  31.1 0.1 reshape.547
  31.2 2.6 multiply_convert_fusion.2
  33.8 0.6 fusion.28
  34.4 1.0 fusion.37
  35.4 0.0 all-gather.7.cloned.1.call-start
  35.6 0.3 copy.179
  35.9 2.6 copy.182
  38.5 3.9 %convert_multiply_fusion = f32[1,768,1024]{1,2,0:T(8,128)} fusion(bf16[1,768,1024]{1,2,0:T(8,128)(2,1)} %copy.182), kind=kLoop, calls=%fused_computation.13 | loop fusion | flops 3932160 | bytes 4718592 | tf_op jit(solution)/shard_map/jit(silu)/mul | solution.py:147
  42.4 6.2 %reshape.560 = f32[1,3,256,2,8,64]{2,1,5,4,3,0:T(4,128)} reshape(f32[1,768,1024]{1,2,0:T(8,128)} %convert_multiply_fusion) | data formatting | bytes 6291456 | tf_op jit(solution)/shard_map/reshape | solution.py:147
  48.6 0.6 mul.497
  49.2 6.7 %all-gather = f32[4,2,8,1]{2,1,3,0:T(2,128)} all-gather(f32[1,2,8,1]{2,1,3,0:T(2,128)S(1)} %copy-done.19), channel_id=2, replica_groups=mesh['dp'=2,'seq'=4,'head'=4] {'seq'}, dimensions={0}, use_global_device_ids=true | all-gather | bytes 320 | tf_op jit(solution)/shard_map/all_gather | solution.py:23
  56.0 0.6 fusion.52
  56.6 0.7 bitcast_add_fusion.5
  57.3 5.6 %reshape.562 = f32[1,3,256,2,8,64]{2,1,5,4,3,0:T(4,128)} reshape(bf16[1,768,1024]{1,2,0:T(8,128)(2,1)} %copy-done.1) | data formatting | bytes 4718592 | tf_op jit(solution)/shard_map/convert_element_type | solution.py:110
  62.9 0.1 copy.155
  62.9 0.1 maximum_convert_fusion.1
  63.1 1.2 multiply_convert_fusion.5
  64.2 0.1 reshape.546
  64.3 1.5 fusion.44
  65.9 7.4 %fusion.1 = f32[3,2,8,64,256]{4,3,2,1,0:T(8,128)} fusion(f32[2,3,256,256]{3,2,0,1:T(8,128)} %fusion.44, pred[256,256]{1,0:T(8,128)(4,1)S(1)} %iota_compare_fusion, bf16[3,256,2,8,64]{1,0,4,3,2:T(4,128)(2,1)} %reshape.545, f32[2,8,3,256]{3,1,2,0:T(8,128)S(1)} %bitcast.161, f32[2,8,3,256]{3,1,2,0:T(8,128)S(1)} %copy-done.9), kind=kOutput, calls=%fused_computation.5 | convolution fusion | flops 421527552 | bytes 6455296 | tf_op jit(solution)/shard_map/rgkcqs,rcsgkp->rcqgkp/dot_general | solution.py:104
  73.3 3.7 %while.16 = (s32[]{:T(128)}, f32[1,2,8]{2,1,0:T(2,128)S(1)}, f32[1,2,8,64,128]{4,3,2,1,0:T(8,128)S(1)}, s32[]{:T(128)}, f32[4,1,2,8]{3,2,1,0:T(2,128)S(1)}, /*in...) while((s32[]{:T(128)}, f32[1,2,8]{2,1,0:T(2,128)S(1)}, ...), condition=%wide.region_3.4_spmd.clone, body=%wide.region_2.3_spmd.clone.sunk | while | flops 524340 | bytes 1573367 | solution.py:32
  73.3 1.2 fusion.59
  74.6 1.2 fusion.59
  75.9 1.2 fusion.59
  77.1 0.2 add_bitcast_fusion
  77.3 0.2 fusion.39
  77.5 1.7 copy-done.2
  79.3 4.7 %fusion.19 = (f32[3,256,2]{1,2,0:T(2,128)S(1)}, f32[1,3,256,2,8,64]{2,5,4,3,1,0:T(8,128)S(1)}) fusion(f32[1,3,256,2,8,64]{2,1,5,4,3,0:T(4,128)S(1)} %copy-done.2, f32[1,3,256,2,8,64]{2,1,5,4,3,0:T(4,128)} %reshape.562, f32[2,8]{1,0:T(2,128)S(1)} %copy-done.16, f32[3,256,2,8]{1,3,2,0:T(8,128)S(1)} %bitcast.163, ...), kind=kOutput, calls=%fused_computation.35 | convolution fusion | flops 1214249472 | bytes 14604352 | tf_op jit(solution)/shard_map/rcqgn,rgkcpn->rcqgkp/dot_general | solution.py:141
  83.9 2.2 copy.181
  86.2 0.8 copy.195
  87.0 0.6 copy-done
  87.5 2.2 fusion.17
  89.8 0.3 all-gather.9.cloned.1.call-start
  90.1 0.5 all-gather.9.cloned.1.call-update
  90.5 115.7 %all-gather.7.cloned.1.call-done = bf16[768,4096]{0,1:T(8,128)(2,1)} async-done(((bf16[768,1024]{0,1:T(8,128)(2,1)}), bf16[768,4096]{0,1:T(8,128)(2,1)}) %all-gather.7.cloned.1.call-update) | async-done | bytes 6291472 | tf_op jit(solution)/shard_map/all_gather | solution.py:158
  206.2 89.5 %all-gather.9.cloned.1.call-done = bf16[4096,2048]{1,0:T(8,128)(2,1)} async-done(((bf16[512,2048]{1,0:T(8,128)(2,1)}), bf16[4096,2048]{1,0:T(8,128)(2,1)}) %all-gather.9.cloned.1.call-update) | async-done | bytes 16777232 | tf_op jit(solution)/shard_map/all_gather | solution.py:159
  295.7 19.8 %fusion.20 = bf16[1,768,2048]{2,1,0:T(8,128)(2,1)} fusion(bf16[768,4096]{0,1:T(8,128)(2,1)} %all-gather.7.cloned.1.call-done, bf16[4096,2048]{1,0:T(8,128)(2,1)} %all-gather.9.cloned.1.call-done), kind=kOutput, calls=%fused_computation.38 | convolution fusion | flops 12886474752 | bytes 26214400 | tf_op jit(solution)/shard_map/dot_general | solution.py:160
  (73 shorter events, 0.5 us)
Async XLA Ops:
  6.5 66.7 %all-gather.5.cloned.1.call-start = ((), (), s32[]{:S(2)}) async-start(), calls=%async_computation | async-start | bytes 2621440 | tf_op jit(solution)/shard_map/all_gather | solution.py:23
  9.6 12.4 %collective-permute-start = (bf16[1,3,1536]{1,2,0:T(8,128)(2,1)}, bf16[1,3,1536]{1,2,0:T(8,128)(2,1)}, u32[]{:S(2)}, u32[]{:S(2)}) collective-permute-start(bf16[1,3,1536]{1,2,0:T(8,128)(2,1)} %copy.153), channel_id=1, source_target_pairs={{0,4},{4,8},{8,12},{1,5},{5,9},{9,13},{2,6},{6,10},{10,14},{3,7},{... | collective-permute-start | bytes 27656 | tf_op jit(solution)/shard_map/ppermute | solution.py:18
  12.4 5.7 %copy-start.13 = (f32[4,1024]{1,0:T(4,128)S(1)}, f32[4,1024]{1,0:T(4,128)}, u32[]{:S(2)}) copy-start(f32[4,1024]{1,0:T(4,128)} %param.23) | copy-start | bytes 49156
  12.4 5.7 %copy-start.20 = (f32[4,256]{1,0:T(4,128)S(1)}, f32[4,256]{1,0:T(4,128)}, u32[]{:S(2)}) copy-start(f32[4,256]{1,0:T(4,128)} %param.24) | copy-start | bytes 12292
  16.2 3.1 copy-start.6
  18.8 15.6 %copy-start.14 = (f32[2,8]{1,0:T(2,128)}, f32[2,8]{1,0:T(2,128)S(1)}, u32[]{:S(2)}) copy-start(f32[2,8]{1,0:T(2,128)S(1)} %get-tuple-element.212) | copy-start | bytes 196
  19.9 14.5 %copy-start.11 = (f32[2,8]{1,0:T(2,128)}, f32[2,8]{1,0:T(2,128)S(1)}, u32[]{:S(2)}) copy-start(f32[2,8]{1,0:T(2,128)S(1)} %get-tuple-element.209) | copy-start | bytes 196
  27.3 3.7 %copy-start.1 = (bf16[1,768,1024]{1,2,0:T(8,128)(2,1)}, bf16[1,768,1024]{1,2,0:T(8,128)(2,1)S(1)}, u32[]{:S(2)}) copy-start(bf16[1,768,1024]{1,2,0:T(8,128)(2,1)S(1)} %multiply_convert_fusion.3) | copy-start | bytes 4718596
  27.3 3.1 copy-start.4
  35.4 170.8 %all-gather.7.cloned.1.call-start = ((), (), s32[]{:S(2)}) async-start(), calls=%async_computation.1 | async-start | bytes 7864320 | tf_op jit(solution)/shard_map/all_gather | solution.py:158
  42.4 6.2 %copy-start.23 = (f32[16]{0:T(128)S(1)}, f32[16]{0:T(128)}, u32[]{:S(2)}) copy-start(f32[16]{0:T(128)} %param.21) | copy-start | bytes 196
  42.4 6.8 %copy-start.19 = (f32[1,2,8,1]{2,1,3,0:T(2,128)S(1)}, f32[1,2,8,1]{2,1,3,0:T(2,128)}, u32[]{:S(2)}) copy-start(f32[1,2,8,1]{2,1,3,0:T(2,128)} %get-tuple-element.211) | copy-start | bytes 196
  42.4 13.6 %copy-start.21 = (f32[4,256]{1,0:T(4,128)S(1)}, f32[4,256]{1,0:T(4,128)}, u32[]{:S(2)}) copy-start(f32[4,256]{1,0:T(4,128)} %param.25) | copy-start | bytes 12292
  42.4 14.2 %copy-start.7 = (f32[2,8,3,2]{1,3,2,0:T(2,128)S(1)}, f32[2,8,3,2]{1,3,2,0:T(2,128)}, u32[]{:S(2)}) copy-start(f32[2,8,3,2]{1,3,2,0:T(2,128)} %copy-done.6) | copy-start | bytes 1156
  48.6 14.4 %copy-start.5 = (bf16[1,768,256]{2,1,0:T(8,128)(2,1)S(1)}, bf16[1,768,256]{2,1,0:T(8,128)(2,1)}, u32[]{:S(2)}) copy-start(bf16[1,768,256]{2,1,0:T(8,128)(2,1)} %param.17) | copy-start | bytes 1179652
  63.1 2.8 copy-start.9
  65.9 7.4 %copy-start.8 = (f32[4,2,8,1]{2,1,3,0:T(2,128)S(1)}, f32[4,2,8,1]{2,1,3,0:T(2,128)}, u32[]{:S(2)}) copy-start(f32[4,2,8,1]{2,1,3,0:T(2,128)} %all-gather) | copy-start | bytes 772
  65.9 7.4 %copy-start.10 = (f32[1,2,8]{2,1,0:T(2,128)S(1)}, f32[1,2,8]{2,1,0:T(2,128)}, u32[]{:S(2)}) copy-start(f32[1,2,8]{2,1,0:T(2,128)} %custom-call) | copy-start | bytes 196
  73.3 3.8 %copy-start.3 = (f32[1,16,64,128]{3,2,1,0:T(8,128)S(1)}, f32[1,16,64,128]{3,2,1,0:T(8,128)}, u32[]{:S(2)}) copy-start(f32[1,16,64,128]{3,2,1,0:T(8,128)} %param.26) | copy-start | bytes 1572868
  73.3 3.8 %copy-start.12 = (f32[2,8]{1,0:T(2,128)S(1)}, f32[2,8]{1,0:T(2,128)}, u32[]{:S(2)}) copy-start(f32[2,8]{1,0:T(2,128)} %copy-done.11) | copy-start | bytes 196
  73.3 3.8 %copy-start.17 = (f32[2,8]{1,0:T(2,128)S(1)}, f32[2,8]{1,0:T(2,128)}, u32[]{:S(2)}) copy-start(f32[2,8]{1,0:T(2,128)} %get-tuple-element.213) | copy-start | bytes 196
  73.3 4.0 %copy-start.15 = (f32[2,8]{1,0:T(2,128)S(1)}, f32[2,8]{1,0:T(2,128)}, u32[]{:S(2)}) copy-start(f32[2,8]{1,0:T(2,128)} %copy-done.14) | copy-start | bytes 196
  73.3 4.0 %copy-start.18 = (f32[2,8]{1,0:T(2,128)S(1)}, f32[2,8]{1,0:T(2,128)}, u32[]{:S(2)}) copy-start(f32[2,8]{1,0:T(2,128)} %get-tuple-element.208) | copy-start | bytes 196
  77.1 2.2 copy-start.2
  77.1 2.2 copy-start.16
  86.1 1.4 copy-start
  86.1 1.4 copy-start.22
  89.8 205.9 %all-gather.9.cloned.1.call-start = ((), (), s32[]{:S(2)}) async-start(), calls=%async_computation.2 | async-start | bytes 18874368 | tf_op jit(solution)/shard_map/all_gather | solution.py:159
Sparse Core Ops, SparseCore 0:
  35.5 23.9 all-gather.4
  89.9 116.2 all-gather.6
  208.1 87.5 all-gather.8
where the time goes:
time: 325 us; the launch traced here: 322 us
  waiting for transfers between devices  206 us (63%)
  matrix products  34 us (10%)
  local copies, waits for them, and re-layouts  32.4 us (10%)
  other arithmetic  27.9 us (9%)
  between operations  13.6 us (4%)
  blocking collectives  6.7 us (2%)
    all_gather x1, waiting for transfers between devices, local(): wide_all = lax.all_gather(normed, 'head', axis=1, tiled=True)  116 us
    all_gather x1, waiting for transfers between devices, local(): full_weight = lax.all_gather(out_weight, ('dp', 'seq'), axis=0, tiled=True)  89.5 us
    dot_general x1, matrix products, local(): jnp.dot(wide_all, full_weight, preferred_element_type=jnp.float32)  19.8 us
    unnamed x51, local copies, waits for them, and re-layouts  7.53 us
    dot_general x1, matrix products, local(): jnp.einsum('rgkcqs,rcsgkp->rcqgkp', mixing, x_shaped, preferred_element_t...  7.36 us
    all_gather x1, blocking collectives, entering(): pieces = jax.tree.map(lambda part: lax.all_gather(part, axis), value)  6.7 us
  transfers between devices with their start and end apart: 4, of which 2 were waited for; matrix products, arithmetic and copies ran while one was open for 13% of the time, Pallas kernels for 0%

commit v1 on v0

v1 whole, which is shorter than its diff:
```python
import functools

import jax
import jax.numpy as jnp
from jax import lax
from jax.experimental import pallas as pl
from jax.experimental.pallas import tpu as pltpu
from jax.sharding import PartitionSpec as P

HEAD_SIZE = 64
STATE = 128
BLOCK_LEN = 256
TAPS = 4
EPSILON = 1e-05
RIM = 16

F32 = jnp.float32
BF16 = jnp.bfloat16
MESH = pl.DeviceIdType.MESH
HIGHEST = lax.Precision.HIGHEST


def dot(a, b, dims=((1,), (0,)), precision=None):
    return lax.dot_general(a, b, (dims, ((), ())), precision=precision, preferred_element_type=F32)


def split(v):
    hi = v.astype(BF16)
    return hi, (v - hi.astype(F32)).astype(BF16)


def silu(v):
    return v / (1.0 + jnp.exp(-v))


def kernel(
    sizes,
    x_hbm, b_hbm, c_hbm, z_hbm, w_hbm, dt_ref, a_ref, skip_ref, gain_ref, kx_ref, kb_ref, kc_ref, init_ref,
    out_ref,
    w_all, n_all, xpad, bpad, cpad, z_v, xc, bc, cc, y_v, states, e_in, e_out, dt_row, cum_row, dt_col, cum_col,
    decay, acc,
    load_sem, halo_send, halo_recv, w_send, w_recv, p_send, e_send, e_recv, up_sem, down_sem, n_recv,
):
    D, S, H = sizes
    T = z_v.shape[0]
    G = n_all.shape[1]
    NB = T // BLOCK_LEN
    R = G * NB
    L = BLOCK_LEN
    heads = dt_row.shape[1]
    per = heads // G
    wide = per * HEAD_SIZE
    rows = w_hbm.shape[0]
    M = w_all.shape[1]
    dp, seq, h = lax.axis_index("dp"), lax.axis_index("seq"), lax.axis_index("head")
    SC = S // 2
    NQ = D * SC
    core = lax.rem(seq, 2)
    q = dp * SC + seq // 2
    me = dp * S + seq
    sibling = seq + 1 - 2 * core

    def local(src, dst, i):
        return pltpu.make_async_copy(src, dst, load_sem.at[i])

    loads = [
        local(x_hbm.at[0], xpad.at[pl.ds(RIM, T)], 0),
        local(b_hbm.at[0], bpad.at[pl.ds(RIM, T)], 1),
        local(c_hbm.at[0], cpad.at[pl.ds(RIM, T)], 2),
        local(z_hbm.at[0], z_v, 3),
        local(w_hbm, w_all.at[pl.ds(pl.multiple_of(me * rows, rows), rows)], 4),
    ]
    for copy in loads:
        copy.start()

    barrier = pltpu.get_barrier_semaphore()
    for k in range(1, D * S):
        other = lax.rem(me + k, D * S)
        pl.semaphore_signal(
            barrier, inc=1, device_id={"dp": other // S, "seq": lax.rem(other, S)}, device_id_type=MESH
        )

    for k in (1, H - 1):
        pl.semaphore_signal(barrier, inc=1, device_id={"head": lax.rem(h + k, H)}, device_id_type=MESH)
    pl.semaphore_wait(barrier, D * S + 1)

    halos = [
        pltpu.make_async_remote_copy(
            src_ref=src.at[0, pl.ds(T - RIM, RIM)],
            dst_ref=dst.at[pl.ds(0, RIM)],
            send_sem=halo_send.at[i],
            recv_sem=halo_recv.at[i],
            device_id={"seq": lax.rem(seq + 1, S)},
            device_id_type=MESH,
        )
        for i, (src, dst) in enumerate(((x_hbm, xpad), (b_hbm, bpad), (c_hbm, cpad)))
    ]
    for copy in halos:

        @pl.when(seq < S - 1)
        def _(copy=copy):
            copy.start()

    def w_rows(owner):
        return w_all.at[pl.ds(pl.multiple_of(owner * rows, rows), rows)]

    def owner_of(chip, on):
        return (chip // SC) * S + lax.rem(chip, SC) * 2 + on

    def w_push(k):
        chip = lax.rem(q + k, NQ)
        return pltpu.make_async_remote_copy(
            src_ref=w_hbm,
            dst_ref=w_rows(me),
            send_sem=w_send.at[k],
            recv_sem=w_recv.at[me],
            device_id={"dp": chip // SC, "seq": lax.rem(chip, SC) * 2 + core},
            device_id_type=MESH,
        )

    def w_pair(k, src=None):
        chip = lax.rem(q + NQ - k, NQ)
        owner = owner_of(chip, core)
        return pltpu.make_async_remote_copy(
            src_ref=w_rows(owner) if src is None else src,
            dst_ref=w_rows(owner),
            send_sem=p_send.at[k],
            recv_sem=w_recv.at[owner],
            device_id={"seq": sibling},
            device_id_type=MESH,
        )

    def w_arrived(owner):
        return pltpu.make_async_remote_copy(
            src_ref=w_hbm,
            dst_ref=w_rows(owner),
            send_sem=w_send.at[0],
            recv_sem=w_recv.at[owner],
            device_id={"seq": sibling},
            device_id_type=MESH,
        )

    first = [k for k in range(1, NQ) if k % SC == 0]
    later = [k for k in range(1, NQ) if k % SC != 0]
    for k in first:
        w_push(k).start()

    lane = lax.broadcasted_iota(jnp.int32, (L, L), 1)
    line = lax.broadcasted_iota(jnp.int32, (L, L), 0)
    eye = jnp.where(lane == line, 1.0, 0.0).astype(F32)
    low = jnp.where(lane <= line, 1.0, 0.0).astype(F32)
    rate = -jnp.exp(a_ref[...])
    for b in range(NB):
        raw = dt_ref[0, :, b * L : (b + 1) * L]
        step = jnp.maximum(raw, 0.0) + jnp.log1p(jnp.exp(-jnp.abs(raw)))
        dt_row[b] = step
        step_c = dot(eye, step, ((1,), (1,)), HIGHEST)
        cum = dot(low, step_c * rate, precision=HIGHEST)
        dt_col[b * L : (b + 1) * L] = step_c
        cum_col[b * L : (b + 1) * L] = cum
        cum_row[b] = dot(cum, eye, ((0,), (0,)), HIGHEST)

    def spread_mat(g):
        head = lax.broadcasted_iota(jnp.int32, (heads, wide), 0)
        chan = lax.broadcasted_iota(jnp.int32, (heads, wide), 1)
        inside = (chan >= (head - g * per) * HEAD_SIZE) & (chan < (head - g * per + 1) * HEAD_SIZE)
        return jnp.where(inside, 1.0, 0.0).astype(BF16)

    def expand(v, mat):
        hi, lo = split(v)
        return dot(hi, mat) + dot(lo, mat)

    for i in range(3):
        loads[i].wait()
    for copy, pad in zip(halos, (xpad, bpad, cpad)):

        @pl.when(seq > 0)
        def _(copy=copy):
            copy.wait_recv()

        @pl.when(seq == 0)
        def _(pad=pad):
            pad[0:RIM] = jnp.zeros((RIM, pad.shape[1]), BF16)

    def conv(pad, taps, dst, b, at):
        v = pad[pl.ds(pl.multiple_of(b * L, L), L + RIM), at : at + 128].astype(F32)
        total = v * taps[TAPS - 1 : TAPS, at : at + 128]
        for back in range(1, TAPS):
            total = total + pltpu.roll(v, back, 0) * taps[TAPS - 1 - back : TAPS - back, at : at + 128]
        dst[pl.ds(pl.multiple_of(b * L, L), L), at : at + 128] = silu(total[RIM:]).astype(BF16)

    def e_copy(g):
        return pltpu.make_async_remote_copy(
            src_ref=e_out.at[g],
            dst_ref=e_in.at[g],
            send_sem=e_send.at[g],
            recv_sem=e_recv.at[g],
            device_id={"seq": lax.rem(seq + 1, S)},
            device_id_type=MESH,
        )

    for g in range(G):
        mat = spread_mat(g)

        def block(b, carry, g=g, mat=mat):
            here = pl.ds(pl.multiple_of(b * L, L), L)
            conv(bpad, kb_ref, bc, b, g * STATE)
            for at in range(g * wide, (g + 1) * wide, 128):
                conv(xpad, kx_ref, xc, b, at)
            cum = cum_col[here]
            last = cum[L - 1 : L]
            weight = expand(jnp.exp(last - cum) * dt_col[here], mat)
            weighted = (weight * xc[here, g * wide : (g + 1) * wide].astype(F32)).astype(BF16)
            states[b, g] = dot(bc[here, g * STATE : (g + 1) * STATE], weighted, ((0,), (0,)))
            decay[b, g] = expand(jnp.broadcast_to(jnp.exp(last), (8, heads)), mat)
            return carry

        lax.fori_loop(0, NB, block, 0)

        @pl.when(seq == 0)
        def _(g=g):
            e_in[g] = init_ref[g * wide : (g + 1) * wide].T

        @pl.when(seq > 0)
        def _(g=g):
            e_copy(g).wait_recv()

        def chain(i, carry, g=g):
            at = pl.ds(pl.multiple_of(i * 32, 32), 32)
            run = e_in[g, at]
            for b in range(NB):
                fresh = states[b, g, at]
                states[b, g, at] = run
                run = decay[b, g, 0:1] * run + fresh
            e_out[g, at] = run
            return carry

        lax.fori_loop(0, STATE // 32, chain, 0)

        @pl.when(seq < S - 1)
        def _(g=g):
            e_copy(g).start()

    for k in later:
        w_push(k).start()
    w_pair(0, w_hbm).start()

    def chunk(s, r):
        return n_all.at[s, r // NB, pl.ds(pl.multiple_of(lax.rem(r, NB) * L, L), L)]

    def pass_up(s, r):
        return pltpu.make_async_remote_copy(
            src_ref=chunk(s, r), dst_ref=chunk(s, r), send_sem=up_sem.at[s, r], recv_sem=n_recv.at[s, r],
            device_id={"head": lax.rem(h + 1, H)}, device_id_type=MESH,
        )

    def pass_down(s, r):
        return pltpu.make_async_remote_copy(
            src_ref=chunk(s, r), dst_ref=chunk(s, r), send_sem=down_sem.at[s, r], recv_sem=n_recv.at[s, r],
            device_id={"head": lax.rem(h + H - 1, H)}, device_id_type=MESH,
        )

    def send_own(r):
        @pl.when(h < H - 1)
        def _():
            pass_up(h, r).start()

        @pl.when(h > 0)
        def _():
            pass_down(h, r).start()

    def forward(r):
        for d in range(1, H - 1):
            back = r - d
            ok = (back >= 0) & (back < R)

            @pl.when(ok & (h - d >= 0) & (h < H - 1))
            def _(d=d, back=back):
                copy = pass_up(h - d, back)
                copy.wait_recv()
                copy.start()

            @pl.when(ok & (h + d < H) & (h > 0))
            def _(d=d, back=back):
                copy = pass_down(h + d, back)
                copy.wait_recv()
                copy.start()

    loads[3].wait()
    side = lax.broadcasted_iota(jnp.int32, (L, 128), 1) < HEAD_SIZE
    for g in range(G):
        mat = spread_mat(g)
        lo, hi = g * wide, (g + 1) * wide

        def round_(b, carry, g=g, mat=mat, lo=lo, hi=hi):
            here = pl.ds(pl.multiple_of(b * L, L), L)
            conv(cpad, kc_ref, cc, b, g * STATE)
            c = cc[here, g * STATE : (g + 1) * STATE]
            scores = dot(c, bc[here, g * STATE : (g + 1) * STATE], ((1,), (1,)))
            rowi = lax.broadcasted_iota(jnp.int32, (L, L), 0)
            coli = lax.broadcasted_iota(jnp.int32, (L, L), 1)
            scores = jnp.where(rowi >= coli, scores, 0.0)
            cum = cum_col[here]
            for pair in range(per // 2):
                at = lo + pair * 128
                u = xc[here, at : at + 128]
                parts = []
                for j in range(2):
                    k = g * per + pair * 2 + j
                    gap = jnp.minimum(cum[:, k : k + 1] - cum_row[b, k : k + 1], 0.0)
                    mixing = (scores * jnp.exp(gap) * dt_row[b, k : k + 1]).astype(BF16)
                    parts.append(dot(mixing, u))
                y_v[:, pair * 128 : (pair + 1) * 128] = jnp.where(side, parts[0], parts[1])
            s_hi, s_lo = split(states[b, g])
            inter = dot(c, s_hi) + dot(c, s_lo)
            skip = expand(jnp.broadcast_to(skip_ref[...], (8, heads)), mat)[0:1]
            y = y_v[...] + inter * expand(jnp.exp(cum), mat) + skip * xc[here, lo:hi].astype(F32)
            gated = y * silu(z_v[here, lo:hi].astype(F32))
            power = jnp.mean(gated * gated, axis=-1, keepdims=True)
            normed = gated * lax.rsqrt(power + EPSILON) * gain_ref[:, lo:hi]
            n_all[h, g, here] = normed.astype(BF16)
            r = g * NB + b
            send_own(r)
            forward(r)
            return carry

        lax.fori_loop(0, NB, round_, 0)

    def drain(r, carry):
        forward(r)
        return carry

    lax.fori_loop(R, R + H - 2, drain, 0)

    for k in first + later:
        w_arrived(owner_of(lax.rem(q + NQ - k, NQ), core)).wait_recv()
        w_pair(k).start()
    loads[4].wait()
    for k in [0] + first + later:
        w_arrived(owner_of(lax.rem(q + NQ - k, NQ), 1 - core)).wait_recv()

    end = (h == 0) | (h == H - 1)
    CT = 512

    def unit(r, carry):
        g, b = r // NB, lax.rem(r, NB)
        here = pl.ds(pl.multiple_of(b * L, L), L)
        for d in range(H):
            s = jnp.where(h == 0, d, lax.rem(h + H - d, H))
            if d > 0:

                @pl.when(end)
                def _(s=s):
                    pass_up(s, r).wait_recv()

            def cols(j, c2, d=d, s=s):
                at = pl.ds(pl.multiple_of(j * CT, CT), CT)
                depth = pl.ds(pl.multiple_of((s * G + g) * wide, wide), wide)
                term = dot(n_all[s, g, here], w_all[depth, at])
                if d == 0:

                    @pl.when(g == 0)
                    def _():
                        acc[here, at] = term

                    @pl.when(g > 0)
                    def _():
                        acc[here, at] += term
                elif d == H - 1:
                    total = acc[here, at] + term

                    @pl.when(g < G - 1)
                    def _():
                        acc[here, at] = total

                    @pl.when(g == G - 1)
                    def _():
                        out_ref[0, here, at] = total.astype(BF16)
                else:
                    acc[here, at] += term
                return c2

            lax.fori_loop(0, M // CT, cols, 0)
        return carry

    lax.fori_loop(0, R, unit, 0)

    for copy in halos:

        @pl.when(seq < S - 1)
        def _(copy=copy):
            copy.wait_send()

    for g in range(G):

        @pl.when(seq < S - 1)
        def _(g=g):
            e_copy(g).wait_send()

    for k in first + later:
        w_push(k).wait_send()
    for k in range(NQ):
        w_pair(k).wait_send()

    def sent(r, carry):
        for s in range(H):

            @pl.when((s <= h) & (h < H - 1))
            def _(s=s):
                pass_up(s, r).wait_send()

            @pl.when((s >= h) & (h > 0))
            def _(s=s):
                pass_down(s, r).wait_send()

        return carry

    lax.fori_loop(0, R, sent, 0)


def local(sizes, x_in, b_in, c_in, z_in, dt_in, a_log, skip_gain, norm_gain, conv_x, conv_b, conv_c, init_state, out_weight):
    D, S, H = sizes
    _, T, wide_x = x_in.shape
    wide_b = b_in.shape[2]
    heads = dt_in.shape[1]
    G = wide_b // STATE
    wide = wide_x // G
    NB = T // BLOCK_LEN
    R = G * NB
    rows, M = out_weight.shape
    depth = rows * D * S
    anyw = pl.BlockSpec(memory_space=pl.ANY)
    vmem = pl.BlockSpec(memory_space=pltpu.VMEM)
    dma = pltpu.SemaphoreType.DMA
    return pl.pallas_call(
        functools.partial(kernel, sizes),
        out_shape=jax.ShapeDtypeStruct((1, T, M), BF16),
        in_specs=[anyw] * 5 + [vmem] * 8,
        out_specs=vmem,
        scratch_shapes=[
            pltpu.VMEM((depth, M), BF16),
            pltpu.VMEM((H, G, T, wide), BF16),
            pltpu.VMEM((RIM + T, wide_x), BF16),
            pltpu.VMEM((RIM + T, wide_b), BF16),
            pltpu.VMEM((RIM + T, wide_b), BF16),
            pltpu.VMEM((T, wide_x), BF16),
            pltpu.VMEM((T, wide_x), BF16),
            pltpu.VMEM((T, wide_b), BF16),
            pltpu.VMEM((T, wide_b), BF16),
            pltpu.VMEM((BLOCK_LEN, wide), F32),
            pltpu.VMEM((NB, G, STATE, wide), F32),
            pltpu.VMEM((G, STATE, wide), F32),
            pltpu.VMEM((G, STATE, wide), F32),
            pltpu.VMEM((NB, heads, BLOCK_LEN), F32),
            pltpu.VMEM((NB, heads, BLOCK_LEN), F32),
            pltpu.VMEM((T, heads), F32),
            pltpu.VMEM((T, heads), F32),
            pltpu.VMEM((NB, G, 8, wide), F32),
            pltpu.VMEM((T, M), F32),
            dma((5,)),
            dma((3,)),
            dma((3,)),
            dma((D * S,)),
            dma((D * S,)),
            dma((D * S,)),
            dma((G,)),
            dma((G,)),
            dma((H, R)),
            dma((H, R)),
            dma((H, R)),
        ],
        compiler_params=pltpu.CompilerParams(
            collective_id=0, has_side_effects=True, vmem_limit_bytes=56 * 1024 * 1024
        ),
        cost_estimate=pl.CostEstimate(flops=2 * T * depth * M, bytes_accessed=depth * M * 2, transcendentals=T * wide_x),
    )(
        x_in, b_in, c_in, z_in, out_weight, dt_in,
        a_log.reshape(1, heads), skip_gain.reshape(1, heads), norm_gain.reshape(1, wide_x),
        conv_x, conv_b, conv_c, init_state.reshape(heads * HEAD_SIZE, STATE),
    )


def solution(mesh):
    sizes = (mesh.shape["dp"], mesh.shape["seq"], mesh.shape["head"])
    in_specs = (
        P("dp", "seq", "head"),
        P("dp", "seq", "head"),
        P("dp", "seq", "head"),
        P("dp", "seq", "head"),
        P("dp", "head", "seq"),
        P("head"),
        P("head"),
        P("head"),
        P(None, "head"),
        P(None, "head"),
        P(None, "head"),
        P("dp", "head", None, None),
        P(("dp", "seq"), "head"),
    )
    out_specs = P("dp", "seq", "head")
    return jax.shard_map(
        functools.partial(local, sizes), mesh=mesh, in_specs=in_specs, out_specs=out_specs, check_vma=False
    )
```

time: 325 us -> 159 us (0.49)
  the two profiles are of different devices: /device:TPU:5 before, /device:TPU:0 now
where the time goes in v1:
time: 159 us
  Pallas kernels  155 us (97%)
  local copies, waits for them, and re-layouts  3.97 us (2%)
    pallas_call x1, Pallas kernels, local(): pl.pallas_call(functools.partial(kernel, sizes), out_shape=jax.ShapeDtype...  155 us
    unnamed x1, local copies, waits for them, and re-layouts  3.97 us

profile of v1, /device:TPU:0, one launch (start us, length us, event | category | flops | bytes accessed | tf_op | source)
XLA Modules:
  0.0 159.2 jit_solution(953191318604944525)
XLA Ops:
  0.0 155.2 %shard_map.127 = bf16[1,768,2048]{2,1,0:T(8,128)(2,1)} custom-call(bf16[1,768,1024]{2,1,0:T(8,128)(2,1)} %x_hbm.1, bf16[1,768,256]{2,1,0:T(8,128)(2,1)} %b_hbm.1, bf16[1,768,256]{2,1,0:T(8,128)(2,1)} %c_hbm.1, bf16[1,768,1024]{2,1,0:T(8,128)(2,1)} %z_hbm.1, bf16[512,2048]{1,0:T(8,128)(2,1)} %w_hbm.1, f32[1,16,768]{2,1,0:T(8,128)} %dt_ref.1, ...), custom_call_target="tpu_custom_call" | custom-call | flops 12884901888 | bytes 16777216 | tf_op jit(solution)/shard_map/pallas_call | solution.py:435
  155.2 4.0 %copy.15 = bf16[1,768,2048]{2,1,0:T(8,128)(2,1)} copy(bf16[1,768,2048]{2,1,0:T(8,128)(2,1)} %shard_map.127) | data formatting | bytes 6291456

commit v2 on v1

--- a/solution.py
+++ b/solution.py
@@ -39,7 +39,7 @@
     out_ref,
     w_all, n_all, xpad, bpad, cpad, z_v, xc, bc, cc, y_v, states, e_in, e_out, dt_row, cum_row, dt_col, cum_col,
     decay, acc,
-    load_sem, halo_send, halo_recv, w_send, w_recv, p_send, e_send, e_recv, up_sem, down_sem, n_recv,
+    load_sem, halo_send, halo_recv, wd_send, wc_send, f_send, w_recv, p_send, e_send, e_recv, up_sem, down_sem, n_recv,
 ):
     D, S, H = sizes
     T = z_v.shape[0]
@@ -54,9 +54,8 @@
     M = w_all.shape[1]
     dp, seq, h = lax.axis_index("dp"), lax.axis_index("seq"), lax.axis_index("head")
     SC = S // 2
-    NQ = D * SC
     core = lax.rem(seq, 2)
-    q = dp * SC + seq // 2
+    spot = seq // 2
     me = dp * S + seq
     sibling = seq + 1 - 2 * core
 
@@ -70,7 +69,7 @@
         local(z_hbm.at[0], z_v, 3),
         local(w_hbm, w_all.at[pl.ds(pl.multiple_of(me * rows, rows), rows)], 4),
     ]
-    for copy in loads:
+    for copy in loads[:4]:
         copy.start()
 
     barrier = pltpu.get_barrier_semaphore()
@@ -101,49 +100,64 @@
         def _(copy=copy):
             copy.start()
 
-    def w_rows(owner):
-        return w_all.at[pl.ds(pl.multiple_of(owner * rows, rows), rows)]
-
-    def owner_of(chip, on):
-        return (chip // SC) * S + lax.rem(chip, SC) * 2 + on
-
-    def w_push(k):
-        chip = lax.rem(q + k, NQ)
+    half = rows // 2
+
+    def w_rows(owner, part=None):
+        if part is None:
+            return w_all.at[pl.ds(pl.multiple_of(owner * rows, rows), rows)]
+        return w_all.at[pl.ds(pl.multiple_of(owner * rows + part * half, half), half)]
+
+    def row_of(i):
+        return lax.rem(dp + D + i, D)
+
+    def spot_of(i):
+        return lax.rem(spot + SC + i, SC)
+
+    def owner_of(i, j, on):
+        return row_of(-i) * S + spot_of(-j) * 2 + on
+
+    def remote(src, dst, send_sem, recv_sem, device_id):
         return pltpu.make_async_remote_copy(
-            src_ref=w_hbm,
-            dst_ref=w_rows(me),
-            send_sem=w_send.at[k],
-            recv_sem=w_recv.at[me],
-            device_id={"dp": chip // SC, "seq": lax.rem(chip, SC) * 2 + core},
-            device_id_type=MESH,
-        )
-
-    def w_pair(k, src=None):
-        chip = lax.rem(q + NQ - k, NQ)
-        owner = owner_of(chip, core)
-        return pltpu.make_async_remote_copy(
-            src_ref=w_rows(owner) if src is None else src,
-            dst_ref=w_rows(owner),
-            send_sem=p_send.at[k],
-            recv_sem=w_recv.at[owner],
-            device_id={"seq": sibling},
-            device_id_type=MESH,
-        )
-
-    def w_arrived(owner):
-        return pltpu.make_async_remote_copy(
-            src_ref=w_hbm,
-            dst_ref=w_rows(owner),
-            send_sem=w_send.at[0],
-            recv_sem=w_recv.at[owner],
-            device_id={"seq": sibling},
-            device_id_type=MESH,
-        )
-
-    first = [k for k in range(1, NQ) if k % SC == 0]
-    later = [k for k in range(1, NQ) if k % SC != 0]
-    for k in first:
-        w_push(k).start()
+            src_ref=src, dst_ref=dst, send_sem=send_sem, recv_sem=recv_sem, device_id=device_id, device_id_type=MESH
+        )
+
+    def push_dp(i):
+        return remote(w_hbm, w_rows(me), wd_send.at[i], w_recv.at[me, 0], {"dp": row_of(i)})
+
+    def push_seq(j):
+        return remote(w_hbm, w_rows(me), wc_send.at[j], w_recv.at[me, 0], {"seq": spot_of(j) * 2 + core})
+
+    def hand_seq(i, j):
+        owner = owner_of(i, 0, core)
+        return remote(
+            w_rows(owner, 0), w_rows(owner, 0), f_send.at[0, i, j], w_recv.at[owner, 0],
+            {"seq": spot_of(j) * 2 + core},
+        )
+
+    def hand_dp(i, j):
+        owner = owner_of(0, j, core)
+        return remote(
+            w_rows(owner, 1), w_rows(owner, 1), f_send.at[1, i, j], w_recv.at[owner, 1], {"dp": row_of(i)}
+        )
+
+    def w_pair(i, j, src=None):
+        owner = owner_of(i, j, core)
+        return remote(
+            w_rows(owner) if src is None else src, w_rows(owner), p_send.at[i, j], w_recv.at[owner, 0],
+            {"seq": sibling},
+        )
+
+    def w_wait(owner, part=None, sem=0):
+        ref = w_rows(owner, part)
+        remote(ref, ref, p_send.at[0, 0], w_recv.at[owner, sem], {"seq": sibling}).wait_recv()
+
+    for i in range(1, D):
+        push_dp(i).start()
+    for j in range(1, SC):
+
+        @pl.when(spot_of(j) < spot)
+        def _(j=j):
+            push_seq(j).start()
 
     lane = lax.broadcasted_iota(jnp.int32, (L, L), 1)
     line = lax.broadcasted_iota(jnp.int32, (L, L), 0)
@@ -241,9 +255,14 @@
         def _(g=g):
             e_copy(g).start()
 
-    for k in later:
-        w_push(k).start()
-    w_pair(0, w_hbm).start()
+    for j in range(1, SC):
+
+        @pl.when(spot_of(j) > spot)
+        def _(j=j):
+            push_seq(j).start()
+
+    w_pair(0, 0, w_hbm).start()
+    loads[4].start()
 
     def chunk(s, r):
         return n_all.at[s, r // NB, pl.ds(pl.multiple_of(lax.rem(r, NB) * L, L), L)]
@@ -269,22 +288,17 @@
         def _():
             pass_down(h, r).start()
 
-    def forward(r):
-        for d in range(1, H - 1):
-            back = r - d
-            ok = (back >= 0) & (back < R)
-
-            @pl.when(ok & (h - d >= 0) & (h < H - 1))
-            def _(d=d, back=back):
-                copy = pass_up(h - d, back)
-                copy.wait_recv()
-                copy.start()
-
-            @pl.when(ok & (h + d < H) & (h > 0))
-            def _(d=d, back=back):
-                copy = pass_down(h + d, back)
-                copy.wait_recv()
-                copy.start()
+    def arrive(d, r, side):
+        s = h - d if side < 0 else h + d
+        copy = (pass_up if side < 0 else pass_down)(s, r)
+        copy.wait_recv()
+
+        @pl.when((h < H - 1) if side < 0 else (h > 0))
+        def _():
+            copy.start()
+
+    def exists(d, side):
+        return (h - d >= 0) if side < 0 else (h + d < H)
 
     loads[3].wait()
     side = lax.broadcasted_iota(jnp.int32, (L, 128), 1) < HEAD_SIZE
@@ -321,69 +335,102 @@
             n_all[h, g, here] = normed.astype(BF16)
             r = g * NB + b
             send_own(r)
-            forward(r)
             return carry
 
         lax.fori_loop(0, NB, round_, 0)
 
-    def drain(r, carry):
-        forward(r)
+    for i in range(1, D):
+        w_wait(owner_of(i, 0, core))
+        for j in range(1, SC):
+            hand_seq(i, j).start()
+        w_pair(i, 0).start()
+    for j in range(1, SC):
+        w_wait(owner_of(0, j, core))
+        for i in range(1, D):
+            hand_dp(i, j).start()
+        w_pair(0, j).start()
+
+    def nearest(r, carry):
+        for side in (-1, 1):
+
+            @pl.when(exists(1, side))
+            def _(side=side):
+                arrive(1, r, side)
+
         return carry
 
-    lax.fori_loop(R, R + H - 2, drain, 0)
-
-    for k in first + later:
-        w_arrived(owner_of(lax.rem(q + NQ - k, NQ), core)).wait_recv()
-        w_pair(k).start()
+    lax.fori_loop(0, R, nearest, 0)
+
+    for i in range(1, D):
+        for j in range(1, SC):
+            owner = owner_of(i, j, core)
+            w_wait(owner, 0, 0)
+            w_wait(owner, 1, 1)
+            w_pair(i, j).start()
     loads[4].wait()
-    for k in [0] + first + later:
-        w_arrived(owner_of(lax.rem(q + NQ - k, NQ), 1 - core)).wait_recv()
-
-    end = (h == 0) | (h == H - 1)
+    for i in range(D):
+        for j in range(SC):
+            w_wait(owner_of(i, j, 1 - core))
+
     CT = 512
 
-    def unit(r, carry):
-        g, b = r // NB, lax.rem(r, NB)
-        here = pl.ds(pl.multiple_of(b * L, L), L)
-        for d in range(H):
-            s = jnp.where(h == 0, d, lax.rem(h + H - d, H))
-            if d > 0:
-
-                @pl.when(end)
-                def _(s=s):
-                    pass_up(s, r).wait_recv()
-
-            def cols(j, c2, d=d, s=s):
-                at = pl.ds(pl.multiple_of(j * CT, CT), CT)
-                depth = pl.ds(pl.multiple_of((s * G + g) * wide, wide), wide)
-                term = dot(n_all[s, g, here], w_all[depth, at])
-                if d == 0:
-
-                    @pl.when(g == 0)
-                    def _():
-                        acc[here, at] = term
-
-                    @pl.when(g > 0)
-                    def _():
-                        acc[here, at] += term
-                elif d == H - 1:
-                    total = acc[here, at] + term
-
-                    @pl.when(g < G - 1)
-                    def _():
-                        acc[here, at] = total
-
-                    @pl.when(g == G - 1)
-                    def _():
-                        out_ref[0, here, at] = total.astype(BF16)
-                else:
+    def product(s, r, fresh=False):
+        g = r // NB
+        here = pl.ds(pl.multiple_of(lax.rem(r, NB) * L, L), L)
+        depth = pl.ds(pl.multiple_of((s * G + g) * wide, wide), wide)
+
+        def cols(j, carry):
+            at = pl.ds(pl.multiple_of(j * CT, CT), CT)
+            term = dot(n_all[s, g, here], w_all[depth, at])
+            if not fresh:
+                acc[here, at] += term
+            else:
+
+                @pl.when(g == 0)
+                def _():
+                    acc[here, at] = term
+
+                @pl.when(g > 0)
+                def _():
                     acc[here, at] += term
-                return c2
-
-            lax.fori_loop(0, M // CT, cols, 0)
+
+            return carry
+
+        lax.fori_loop(0, M // CT, cols, 0)
+
+    def near(r, carry):
+        product(h, r, True)
+        for d in range(1, H - 1):
+            for side in (-1, 1):
+
+                @pl.when(exists(d, side))
+                def _(d=d, side=side):
+                    if d > 1:
+                        arrive(d, r, side)
+                    product(h + side * d, r)
+
         return carry
 
-    lax.fori_loop(0, R, unit, 0)
+    lax.fori_loop(0, R, near, 0)
+
+    def far(r, carry):
+        for side in (-1, 1):
+
+            @pl.when(exists(H - 1, side))
+            def _(side=side):
+                if H > 2:
+                    arrive(H - 1, r, side)
+                product(h + side * (H - 1), r)
+
+        @pl.when(r >= R - NB)
+        def _():
+            here = pl.ds(pl.multiple_of(lax.rem(r, NB) * L, L), L)
+            for at in range(0, M, CT):
+                out_ref[0, here, at : at + CT] = acc[here, at : at + CT].astype(BF16)
+
+        return carry
+
+    lax.fori_loop(0, R, far, 0)
 
     for copy in halos:
 
@@ -397,10 +444,16 @@
         def _(g=g):
             e_copy(g).wait_send()
 
-    for k in first + later:
-        w_push(k).wait_send()
-    for k in range(NQ):
-        w_pair(k).wait_send()
+    for i in range(D):
+        for j in range(SC):
+            w_pair(i, j).wait_send()
+            if i > 0 and j > 0:
+                hand_seq(i, j).wait_send()
+                hand_dp(i, j).wait_send()
+    for i in range(1, D):
+        push_dp(i).wait_send()
+    for j in range(1, SC):
+        push_seq(j).wait_send()
 
     def sent(r, carry):
         for s in range(H):
@@ -460,9 +513,11 @@
             dma((5,)),
             dma((3,)),
             dma((3,)),
-            dma((D * S,)),
-            dma((D * S,)),
-            dma((D * S,)),
+            dma((D,)),
+            dma((S // 2,)),
+            dma((2, D, S // 2)),
+            dma((D * S, 2)),
+            dma((D, S // 2)),
             dma((G,)),
             dma((G,)),
             dma((H, R)),

time: 159 us -> 139 us (0.87)
  the two profiles are of different devices: /device:TPU:0 before, /device:TPU:5 now
where the time goes in v2:
time: 139 us
  Pallas kernels  135 us (97%)
  local copies, waits for them, and re-layouts  3.97 us (3%)
    pallas_call x1, Pallas kernels, local(): pl.pallas_call(functools.partial(kernel, sizes), out_shape=jax.ShapeDtype...  135 us
    unnamed x1, local copies, waits for them, and re-layouts  3.97 us

profile of v2, /device:TPU:5, one launch (start us, length us, event | category | flops | bytes accessed | tf_op | source)
XLA Modules:
  0.0 138.9 jit_solution(10712738635264447287)
XLA Ops:
  0.0 135.0 %shard_map.127 = bf16[1,768,2048]{2,1,0:T(8,128)(2,1)} custom-call(bf16[1,768,1024]{2,1,0:T(8,128)(2,1)} %x_hbm.1, bf16[1,768,256]{2,1,0:T(8,128)(2,1)} %b_hbm.1, bf16[1,768,256]{2,1,0:T(8,128)(2,1)} %c_hbm.1, bf16[1,768,1024]{2,1,0:T(8,128)(2,1)} %z_hbm.1, bf16[512,2048]{1,0:T(8,128)(2,1)} %w_hbm.1, f32[1,16,768]{2,1,0:T(8,128)} %dt_ref.1, ...), custom_call_target="tpu_custom_call" | custom-call | flops 12884901888 | bytes 16777216 | tf_op jit(solution)/shard_map/pallas_call | solution.py:488
  135.0 4.0 %copy.15 = bf16[1,768,2048]{2,1,0:T(8,128)(2,1)} copy(bf16[1,768,2048]{2,1,0:T(8,128)(2,1)} %shard_map.127) | data formatting | bytes 6291456

commit v3 on v2

--- a/solution.py
+++ b/solution.py
@@ -213,6 +213,44 @@
             device_id_type=MESH,
         )
 
+    def chunk(s, r):
+        return n_all.at[s, r // NB, pl.ds(pl.multiple_of(lax.rem(r, NB) * L, L), L)]
+
+    def pass_up(s, r):
+        return pltpu.make_async_remote_copy(
+            src_ref=chunk(s, r), dst_ref=chunk(s, r), send_sem=up_sem.at[s, r], recv_sem=n_recv.at[s, r],
+            device_id={"head": lax.rem(h + 1, H)}, device_id_type=MESH,
+        )
+
+    def pass_down(s, r):
+        return pltpu.make_async_remote_copy(
+            src_ref=chunk(s, r), dst_ref=chunk(s, r), send_sem=down_sem.at[s, r], recv_sem=n_recv.at[s, r],
+            device_id={"head": lax.rem(h + H - 1, H)}, device_id_type=MESH,
+        )
+
+    def send_own(r):
+        @pl.when(h < H - 1)
+        def _():
+            pass_up(h, r).start()
+
+        @pl.when(h > 0)
+        def _():
+            pass_down(h, r).start()
+
+    def arrive(d, r, side):
+        s = h - d if side < 0 else h + d
+        copy = (pass_up if side < 0 else pass_down)(s, r)
+        copy.wait_recv()
+
+        @pl.when((h < H - 1) if side < 0 else (h > 0))
+        def _():
+            copy.start()
+
+    def exists(d, side):
+        return (h - d >= 0) if side < 0 else (h + d < H)
+
+    loads[3].wait()
+    side = lax.broadcasted_iota(jnp.int32, (L, 128), 1) < HEAD_SIZE
     for g in range(G):
         mat = spread_mat(g)
 
@@ -255,55 +293,6 @@
         def _(g=g):
             e_copy(g).start()
 
-    for j in range(1, SC):
-
-        @pl.when(spot_of(j) > spot)
-        def _(j=j):
-            push_seq(j).start()
-
-    w_pair(0, 0, w_hbm).start()
-    loads[4].start()
-
-    def chunk(s, r):
-        return n_all.at[s, r // NB, pl.ds(pl.multiple_of(lax.rem(r, NB) * L, L), L)]
-
-    def pass_up(s, r):
-        return pltpu.make_async_remote_copy(
-            src_ref=chunk(s, r), dst_ref=chunk(s, r), send_sem=up_sem.at[s, r], recv_sem=n_recv.at[s, r],
-            device_id={"head": lax.rem(h + 1, H)}, device_id_type=MESH,
-        )
-
-    def pass_down(s, r):
-        return pltpu.make_async_remote_copy(
-            src_ref=chunk(s, r), dst_ref=chunk(s, r), send_sem=down_sem.at[s, r], recv_sem=n_recv.at[s, r],
-            device_id={"head": lax.rem(h + H - 1, H)}, device_id_type=MESH,
-        )
-
-    def send_own(r):
-        @pl.when(h < H - 1)
-        def _():
-            pass_up(h, r).start()
-
-        @pl.when(h > 0)
-        def _():
-            pass_down(h, r).start()
-
-    def arrive(d, r, side):
-        s = h - d if side < 0 else h + d
-        copy = (pass_up if side < 0 else pass_down)(s, r)
-        copy.wait_recv()
-
-        @pl.when((h < H - 1) if side < 0 else (h > 0))
-        def _():
-            copy.start()
-
-    def exists(d, side):
-        return (h - d >= 0) if side < 0 else (h + d < H)
-
-    loads[3].wait()
-    side = lax.broadcasted_iota(jnp.int32, (L, 128), 1) < HEAD_SIZE
-    for g in range(G):
-        mat = spread_mat(g)
         lo, hi = g * wide, (g + 1) * wide
 
         def round_(b, carry, g=g, mat=mat, lo=lo, hi=hi):
@@ -339,27 +328,37 @@
 
         lax.fori_loop(0, NB, round_, 0)
 
+        if g == 0:
+            for j in range(1, SC):
+
+                @pl.when(spot_of(j) > spot)
+                def _(j=j):
+                    push_seq(j).start()
+
+            w_pair(0, 0, w_hbm).start()
+            loads[4].start()
+
     for i in range(1, D):
         w_wait(owner_of(i, 0, core))
         for j in range(1, SC):
             hand_seq(i, j).start()
         w_pair(i, 0).start()
+    def nearest(r, carry):
+        for side in (-1, 1):
+
+            @pl.when(exists(1, side))
+            def _(side=side):
+                arrive(1, r, side)
+
+        return carry
+
+    lax.fori_loop(0, R, nearest, 0)
+
     for j in range(1, SC):
         w_wait(owner_of(0, j, core))
         for i in range(1, D):
             hand_dp(i, j).start()
         w_pair(0, j).start()
-
-    def nearest(r, carry):
-        for side in (-1, 1):
-
-            @pl.when(exists(1, side))
-            def _(side=side):
-                arrive(1, r, side)
-
-        return carry
-
-    lax.fori_loop(0, R, nearest, 0)
 
     for i in range(1, D):
         for j in range(1, SC):
@@ -374,9 +373,7 @@
 
     CT = 512
 
-    def product(s, r, fresh=False):
-        g = r // NB
-        here = pl.ds(pl.multiple_of(lax.rem(r, NB) * L, L), L)
+    def product(s, g, here, CT, fresh=False):
         depth = pl.ds(pl.multiple_of((s * G + g) * wide, wide), wide)
 
         def cols(j, carry):
@@ -398,33 +395,35 @@
 
         lax.fori_loop(0, M // CT, cols, 0)
 
-    def near(r, carry):
-        product(h, r, True)
+    def near(g, carry):
+        here = pl.ds(0, T)
+        product(h, g, here, 256, True)
         for d in range(1, H - 1):
             for side in (-1, 1):
 
                 @pl.when(exists(d, side))
                 def _(d=d, side=side):
                     if d > 1:
-                        arrive(d, r, side)
-                    product(h + side * d, r)
+                        for b in range(NB):
+                            arrive(d, g * NB + b, side)
+                    product(h + side * d, g, here, 256)
 
         return carry
 
-    lax.fori_loop(0, R, near, 0)
+    lax.fori_loop(0, G, near, 0)
 
     def far(r, carry):
+        here = pl.ds(pl.multiple_of(lax.rem(r, NB) * L, L), L)
         for side in (-1, 1):
 
             @pl.when(exists(H - 1, side))
             def _(side=side):
                 if H > 2:
                     arrive(H - 1, r, side)
-                product(h + side * (H - 1), r)
+                product(h + side * (H - 1), r // NB, here, CT)
 
         @pl.when(r >= R - NB)
         def _():
-            here = pl.ds(pl.multiple_of(lax.rem(r, NB) * L, L), L)
             for at in range(0, M, CT):
                 out_ref[0, here, at : at + CT] = acc[here, at : at + CT].astype(BF16)
 

time: 139 us -> 171 us (1.23)
  Pallas kernels: 135 us -> 167 us
    pallas_call x1, Pallas kernels: 135 us -> 167 us  [local(): pl.pallas_call(functools.partial(kernel, sizes), out_shape=jax.ShapeDtype...]
where the time goes in v3:
time: 171 us
  Pallas kernels  167 us (98%)
  local copies, waits for them, and re-layouts  3.97 us (2%)
    pallas_call x1, Pallas kernels, local(): pl.pallas_call(functools.partial(kernel, sizes), out_shape=jax.ShapeDtype...  167 us
    unnamed x1, local copies, waits for them, and re-layouts  3.97 us

profile of v3, /device:TPU:5, one launch (start us, length us, event | category | flops | bytes accessed | tf_op | source)
XLA Modules:
  0.0 171.0 jit_solution(6626390900900880920)
XLA Ops:
  0.0 167.0 %shard_map.127 = bf16[1,768,2048]{2,1,0:T(8,128)(2,1)} custom-call(bf16[1,768,1024]{2,1,0:T(8,128)(2,1)} %x_hbm.1, bf16[1,768,256]{2,1,0:T(8,128)(2,1)} %b_hbm.1, bf16[1,768,256]{2,1,0:T(8,128)(2,1)} %c_hbm.1, bf16[1,768,1024]{2,1,0:T(8,128)(2,1)} %z_hbm.1, bf16[512,2048]{1,0:T(8,128)(2,1)} %w_hbm.1, f32[1,16,768]{2,1,0:T(8,128)} %dt_ref.1, ...), custom_call_target="tpu_custom_call" | custom-call | flops 12884901888 | bytes 16777216 | tf_op jit(solution)/shard_map/pallas_call | solution.py:487
  167.0 4.0 %copy.15 = bf16[1,768,2048]{2,1,0:T(8,128)(2,1)} copy(bf16[1,768,2048]{2,1,0:T(8,128)(2,1)} %shard_map.127) | data formatting | bytes 6291456
